TPU v7x, 256 devices: a whole 4x4x8 slice. The times are simulated.
256 devices in a mesh: leaf: 64 (over y, x, z_lo), panel: 4 (over z_hi, core).
Axes of the slice: x: 4, y: 4, z: 8 (z_hi: 2, z_lo: 4; z = z_hi * 4 + z_lo), core: 2. Of those that a mesh axis runs over, the one named last changes fastest.
Arguments:
- child_front: bfloat16 [16384, 16384], P('leaf', 'panel'), may hold values from -6 to 6
- own_map: int32 [3, 64, 2], P(None, 'leaf'), may hold values from 0 to 1, each once within a row
- cross_map: int32 [3, 64, 2], P(None, 'leaf'), may hold values from 0 to 1, each once within a row
- pivot_inverse: bfloat16 [7, 512, 512], replicated, may hold values from -0.0029296875 to 0.0029296875
Outputs:
- schur: bfloat16 [16384, 16384], P('leaf', 'panel')
Inputs may be any that keep to these rules, and one draw needn't show every extreme that they name: Each own_map[k, d, :] is a permutation of the 2 blocks. Each cross_map[k, d, :] is a permutation of the 2 blocks.
All inputs are finite; a program needn't handle non-finite values.
Results may differ from a plain program's by a relative error of at most 0.0088.
Values may be sent and summed in bfloat16 or wider, within the bound.
A program may use at most 64 MiB of HBM per device.

v0:
```python
import jax
import jax.numpy as jnp
from jax import lax
from jax.sharding import PartitionSpec as P

PANEL = 512
BLOCK = 128


def swapped(block, axis, stride):
    count = lax.axis_size(axis)
    route = []
    for low in range(count):
        high = low | 1 << stride
        if high != low and high < count:
            route += [(low, high), (high, low)]
    return lax.ppermute(block, axis, route)


def spread(block, axis, owner):
    block = jnp.where(lax.axis_index(axis) == owner, block, jnp.zeros_like(block))
    return lax.psum(block, axis)


def extend_add(front_slab, partner, own_index, cross_index, block_count):
    slab_cols = front_slab.shape[1]
    slots = jnp.arange(block_count, dtype=jnp.int32)[None, :]
    own_table = (own_index[:, None] == slots).astype(jnp.bfloat16)
    cross_table = (cross_index[:, None] == slots).astype(jnp.bfloat16)
    own_blocks = front_slab.reshape(block_count, BLOCK, slab_cols)
    cross_blocks = partner.reshape(block_count, BLOCK, slab_cols)
    summed = jnp.einsum("sb,brc->src", own_table, own_blocks, preferred_element_type=jnp.float32)
    summed = summed + jnp.einsum(
        "sb,brc->src", cross_table, cross_blocks, preferred_element_type=jnp.float32
    )
    return summed.reshape(block_count * BLOCK, slab_cols).astype(jnp.bfloat16)


def collect_pivots(own_rows, leaf_index, group_bits):
    buffer = own_rows
    for step_bit in range(group_bits):
        received = swapped(buffer, "leaf", step_bit)
        upper_half = leaf_index >> step_bit & 1 == 1
        buffer = jnp.where(
            upper_half,
            jnp.concatenate([received, buffer], axis=0),
            jnp.concatenate([buffer, received], axis=0),
        )
    return buffer


def top_upper(own_rows, inverse, leaf_index, leaf_bits):
    pivots = collect_pivots(own_rows, leaf_index, leaf_bits)
    product = jnp.dot(inverse, pivots, preferred_element_type=jnp.float32)
    return product.astype(jnp.bfloat16)


def on_device(child_front, own_map, cross_map, pivot_inverse):
    leaf_count = lax.axis_size("leaf")
    leaf_bits = leaf_count.bit_length() - 1
    leaf_index = lax.axis_index("leaf")
    slab_rows = child_front.shape[0]
    block_count = slab_rows // BLOCK
    front_slab = child_front
    offsets = (0, 4, 6)
    for level_index in range(3):
        group_size = leaf_count // 2 ** (2 - level_index)
        group_bits = leaf_bits - 2 + level_index
        share_rows = PANEL // group_size
        partner = swapped(front_slab, "leaf", group_bits - 1)
        parent = extend_add(
            front_slab, partner, own_map[level_index, 0], cross_map[level_index, 0], block_count
        )
        front_number = offsets[level_index] + leaf_index // group_size
        inverse = lax.dynamic_index_in_dim(pivot_inverse, front_number, 0, keepdims=False)
        own_rows = parent[:share_rows]
        if level_index < 2:
            pivots = collect_pivots(own_rows, leaf_index, group_bits)
            upper_rows = jnp.dot(inverse, pivots, preferred_element_type=jnp.float32).astype(
                jnp.bfloat16
            )
        else:
            upper_rows = top_upper(own_rows, inverse, leaf_index, leaf_bits)
        columns = spread(parent[:, :PANEL], "panel", 0)
        reduced = parent.astype(jnp.float32) - jnp.dot(
            columns, upper_rows, preferred_element_type=jnp.float32
        )
        keep_mask = jnp.arange(slab_rows, dtype=jnp.int32)[:, None] >= share_rows
        front_slab = jnp.where(keep_mask, reduced, jnp.zeros_like(reduced)).astype(jnp.bfloat16)
    return front_slab


def solution(mesh):
    placed = (P("leaf", "panel"), P(None, "leaf", None), P(None, "leaf", None), P())
    return jax.shard_map(
        on_device, mesh=mesh, in_specs=placed, out_specs=P("leaf", "panel"), check_vma=False
    )
```

profile of v0, /device:TPU:1, one launch (start us, length us, event | category | flops | bytes accessed | tf_op | source)
XLA Modules:
  0.0 538.7 jit_solution(12298717727944464459)
XLA Ops:
  6.5 3.6 collective-permute-start
  12.1 4.0 fusion.34
  16.2 38.6 %collective-permute-done = bf16[256,4096]{1,0:T(8,128)(2,1)S(1)} collective-permute-done((bf16[256,4096]{1,0:T(8,128)(2,1)}, bf16[256,4096]{1,0:T(8,128)(2,1)S(1)}, u32[]{:S(2)}, u32[]{:S(2)}) %collective-permute-start) | collective-permute-done | bytes 2097184 | tf_op jit(solution)/shard_map/ppermute | solution.py:17
  54.7 3.0 fusion.6
  59.1 2.6 collective-permute-start.1
  61.7 5.1 collective-permute-done.1
  66.9 3.0 collective-permute-start.2
  69.9 22.6 %collective-permute-done.2 = bf16[64,4096]{1,0:T(8,128)(2,1)} collective-permute-done((bf16[64,4096]{1,0:T(8,128)(2,1)S(1)}, bf16[64,4096]{1,0:T(8,128)(2,1)}, u32[]{:S(2)}, u32[]{:S(2)}) %collective-permute-start.2) | collective-permute-done | bytes 524320 | tf_op jit(solution)/shard_map/ppermute | solution.py:17
  95.7 22.0 %collective-permute-done.3 = bf16[128,4096]{1,0:T(8,128)(2,1)} collective-permute-done((bf16[128,4096]{1,0:T(8,128)(2,1)S(1)}, bf16[128,4096]{1,0:T(8,128)(2,1)}, u32[]{:S(2)}, u32[]{:S(2)}) %collective-permute-start.3) | collective-permute-done | bytes 1048608 | tf_op jit(solution)/shard_map/ppermute | solution.py:17
  117.7 3.4 maximum_select_fusion.12
  121.1 2.8 collective-permute-start.4
  124.7 57.9 %all-reduce.4.cloned.1.call-done = bf16[256,512]{1,0:T(8,128)(2,1)} async-done(((bf16[256,512]{1,0:T(8,128)(2,1)}), bf16[256,512]{1,0:T(8,128)(2,1)}) %all-reduce.4.cloned.1.call-update) | async-done | bytes 262160 | tf_op jit(solution)/shard_map/psum | solution.py:22
  182.6 7.2 %fusion.5 = bf16[256,4096]{1,0:T(8,128)(2,1)} fusion(bf16[256,512]{1,0:T(8,128)(2,1)} %all-reduce.4.cloned.1.call-done, bf16[256,4096]{1,0:T(8,128)(2,1)S(1)} %bitcast.44, bf16[256,4096]{1,0:T(8,128)(2,1)} %maximum_select_fusion.12, bf16[256,4096]{1,0:T(8,128)(2,1)} %collective-permute-done.4, pred[]{:T(512)S(6)} %eq.139, ...), kind=kOutput, calls=%fused_computation.14 | convolution fusion | flops 3246391296 | bytes 9175301 | tf_op jit(solution)/shard_map/dot_general | solution.py:85
  190.5 4.1 fusion.31
  194.5 43.1 %collective-permute-done.5 = bf16[256,4096]{1,0:T(8,128)(2,1)S(1)} collective-permute-done((bf16[256,4096]{1,0:T(8,128)(2,1)}, bf16[256,4096]{1,0:T(8,128)(2,1)S(1)}, u32[]{:S(2)}, u32[]{:S(2)}) %collective-permute-start.5) | collective-permute-done | bytes 2097184 | tf_op jit(solution)/shard_map/ppermute | solution.py:17
  237.6 3.0 fusion.7
  242.0 4.5 collective-permute-done.6
  246.7 14.7 %collective-permute-done.7 = bf16[32,4096]{1,0:T(8,128)(2,1)S(1)} collective-permute-done((bf16[32,4096]{1,0:T(8,128)(2,1)S(1)}, bf16[32,4096]{1,0:T(8,128)(2,1)S(1)}, u32[]{:S(2)}, u32[]{:S(2)}) %collective-permute-start.7) | collective-permute-done | bytes 262176 | tf_op jit(solution)/shard_map/ppermute | solution.py:17
  261.6 13.0 %collective-permute-done.8 = bf16[64,4096]{1,0:T(8,128)(2,1)S(1)} collective-permute-done((bf16[64,4096]{1,0:T(8,128)(2,1)S(1)}, bf16[64,4096]{1,0:T(8,128)(2,1)S(1)}, u32[]{:S(2)}, u32[]{:S(2)}) %collective-permute-start.8) | collective-permute-done | bytes 524320 | tf_op jit(solution)/shard_map/ppermute | solution.py:17
  275.9 23.7 %collective-permute-done.9 = bf16[128,4096]{1,0:T(8,128)(2,1)S(1)} collective-permute-done((bf16[128,4096]{1,0:T(8,128)(2,1)S(1)}, bf16[128,4096]{1,0:T(8,128)(2,1)S(1)}, u32[]{:S(2)}, u32[]{:S(2)}) %collective-permute-start.9) | collective-permute-done | bytes 1048608 | tf_op jit(solution)/shard_map/ppermute | solution.py:17
  302.5 52.4 %all-reduce.6.cloned.1.call-done = bf16[256,512]{1,0:T(8,128)(2,1)} async-done(((bf16[256,512]{1,0:T(8,128)(2,1)}), bf16[256,512]{1,0:T(8,128)(2,1)}) %all-reduce.6.cloned.1.call-update) | async-done | bytes 262160 | tf_op jit(solution)/shard_map/psum | solution.py:22
  354.9 7.2 %fusion.4 = bf16[256,4096]{1,0:T(8,128)(2,1)} fusion(bf16[256,512]{1,0:T(8,128)(2,1)} %all-reduce.6.cloned.1.call-done, bf16[256,4096]{1,0:T(8,128)(2,1)S(1)} %bitcast.47, bf16[256,4096]{1,0:T(8,128)(2,1)} %maximum_select_fusion.13, bf16[256,4096]{1,0:T(8,128)(2,1)} %collective-permute-done.10, pred[]{:T(512)S(6)} %eq.147, ...), kind=kOutput, calls=%fused_computation.13 | convolution fusion | flops 3246391296 | bytes 9175301 | tf_op jit(solution)/shard_map/dot_general | solution.py:85
  364.3 4.1 fusion.28
  368.3 42.9 %collective-permute-done.11 = bf16[256,4096]{1,0:T(8,128)(2,1)S(1)} collective-permute-done((bf16[256,4096]{1,0:T(8,128)(2,1)}, bf16[256,4096]{1,0:T(8,128)(2,1)S(1)}, u32[]{:S(2)}, u32[]{:S(2)}) %collective-permute-start.11) | collective-permute-done | bytes 2097184 | tf_op jit(solution)/shard_map/ppermute | solution.py:17
  411.2 3.0 fusion.8
  415.7 3.1 collective-permute-done.12
  418.9 8.4 %collective-permute-done.13 = bf16[16,4096]{1,0:T(8,128)(2,1)S(1)} collective-permute-done((bf16[16,4096]{1,0:T(8,128)(2,1)S(1)}, bf16[16,4096]{1,0:T(8,128)(2,1)S(1)}, u32[]{:S(2)}, u32[]{:S(2)}) %collective-permute-start.13) | collective-permute-done | bytes 131104 | tf_op jit(solution)/shard_map/ppermute | solution.py:17
  427.5 6.9 %collective-permute-done.14 = bf16[32,4096]{1,0:T(8,128)(2,1)S(1)} collective-permute-done((bf16[32,4096]{1,0:T(8,128)(2,1)S(1)}, bf16[32,4096]{1,0:T(8,128)(2,1)S(1)}, u32[]{:S(2)}, u32[]{:S(2)}) %collective-permute-start.14) | collective-permute-done | bytes 262176 | tf_op jit(solution)/shard_map/ppermute | solution.py:17
  434.9 12.7 %collective-permute-done.15 = bf16[64,4096]{1,0:T(8,128)(2,1)S(1)} collective-permute-done((bf16[64,4096]{1,0:T(8,128)(2,1)S(1)}, bf16[64,4096]{1,0:T(8,128)(2,1)S(1)}, u32[]{:S(2)}, u32[]{:S(2)}) %collective-permute-start.15) | collective-permute-done | bytes 524320 | tf_op jit(solution)/shard_map/ppermute | solution.py:17
  448.0 21.9 %collective-permute-done.16 = bf16[128,4096]{1,0:T(8,128)(2,1)S(1)} collective-permute-done((bf16[128,4096]{1,0:T(8,128)(2,1)S(1)}, bf16[128,4096]{1,0:T(8,128)(2,1)S(1)}, u32[]{:S(2)}, u32[]{:S(2)}) %collective-permute-start.16) | collective-permute-done | bytes 1048608 | tf_op jit(solution)/shard_map/ppermute | solution.py:17
  472.6 52.5 %all-reduce.8.cloned.1.call-done = bf16[256,512]{1,0:T(8,128)(2,1)} async-done(((bf16[256,512]{1,0:T(8,128)(2,1)}), bf16[256,512]{1,0:T(8,128)(2,1)}) %all-reduce.8.cloned.1.call-update) | async-done | bytes 262160 | tf_op jit(solution)/shard_map/psum | solution.py:22
  525.1 7.1 %fusion.3 = bf16[256,4096]{1,0:T(8,128)(2,1)} fusion(bf16[256,512]{1,0:T(8,128)(2,1)} %all-reduce.8.cloned.1.call-done, bf16[256,4096]{1,0:T(8,128)(2,1)S(1)} %bitcast.50, bf16[256,4096]{1,0:T(8,128)(2,1)} %maximum_select_fusion.14, bf16[256,4096]{1,0:T(8,128)(2,1)} %collective-permute-done.17, pred[]{:T(512)S(6)} %eq.152, ...), kind=kOutput, calls=%fused_computation.12 | convolution fusion | flops 3246391296 | bytes 9175301 | tf_op jit(solution)/shard_map/dot_general | solution.py:85
  (50 shorter events, 21.5 us)
Async XLA Ops:
  6.5 176.1 %all-reduce.4.cloned.1.call-start = ((), (), s32[]{:S(2)}) async-start(), calls=%async_computation | async-start | bytes 524288 | tf_op jit(solution)/shard_map/psum | solution.py:22
  6.5 48.2 %collective-permute-start = (bf16[256,4096]{1,0:T(8,128)(2,1)}, bf16[256,4096]{1,0:T(8,128)(2,1)S(1)}, u32[]{:S(2)}, u32[]{:S(2)}) collective-permute-start(bf16[256,4096]{1,0:T(8,128)(2,1)} %param.4), channel_id=1, source_target_pairs={{0,32},{32,0},{4,36},{36,4},{8,40},{40,8},{12,44},{44,12},{16,48},... | collective-permute-start | bytes 6291464 | tf_op jit(solution)/shard_map/ppermute | solution.py:17
  59.1 7.7 %collective-permute-start.1 = (bf16[32,4096]{1,0:T(8,128)(2,1)S(1)}, bf16[32,4096]{1,0:T(8,128)(2,1)S(1)}, u32[]{:S(2)}, u32[]{:S(2)}) collective-permute-start(bf16[32,4096]{1,0:T(8,128)(2,1)S(1)} %slice.49), channel_id=1, source_target_pairs={{0,4},{4,0},{8,12},{12,8},{16,20},{20,16},{24,28},{28,24},{32,36},... | collective-permute-start | bytes 786440 | tf_op jit(solution)/shard_map/ppermute | solution.py:17
  66.9 3.0 copy-start
  66.9 25.6 %collective-permute-start.2 = (bf16[64,4096]{1,0:T(8,128)(2,1)S(1)}, bf16[64,4096]{1,0:T(8,128)(2,1)}, u32[]{:S(2)}, u32[]{:S(2)}) collective-permute-start(bf16[64,4096]{1,0:T(8,128)(2,1)S(1)} %maximum_select_fusion.18), channel_id=1, source_target_pairs={{0,8},{8,0},{4,12},{12,4},{16,24},{24,16},{20,28},{28,20},{32,40},... | collective-permute-start | bytes 1572872 | tf_op jit(solution)/shard_map/ppermute | solution.py:17
  94.4 23.3 %collective-permute-start.3 = (bf16[128,4096]{1,0:T(8,128)(2,1)S(1)}, bf16[128,4096]{1,0:T(8,128)(2,1)}, u32[]{:S(2)}, u32[]{:S(2)}) collective-permute-start(bf16[128,4096]{1,0:T(8,128)(2,1)S(1)} %maximum_select_fusion.15), channel_id=1, source_target_pairs={{0,16},{16,0},{4,20},{20,4},{8,24},{24,8},{12,28},{28,12},{32,48},... | collective-permute-start | bytes 3145736 | tf_op jit(solution)/shard_map/ppermute | solution.py:17
  121.1 61.5 %collective-permute-start.4 = (bf16[256,4096]{1,0:T(8,128)(2,1)}, bf16[256,4096]{1,0:T(8,128)(2,1)}, u32[]{:S(2)}, u32[]{:S(2)}) collective-permute-start(bf16[256,4096]{1,0:T(8,128)(2,1)} %maximum_select_fusion.12), channel_id=1, source_target_pairs={{0,32},{32,0},{4,36},{36,4},{8,40},{40,8},{12,44},{44,12},{16,48},... | collective-permute-start | bytes 6291464 | tf_op jit(solution)/shard_map/ppermute | solution.py:17
  124.6 230.2 %all-reduce.6.cloned.1.call-start = ((), (), s32[]{:S(2)}) async-start(), calls=%async_computation.1 | async-start | bytes 524288 | tf_op jit(solution)/shard_map/psum | solution.py:22
  189.9 47.7 %collective-permute-start.5 = (bf16[256,4096]{1,0:T(8,128)(2,1)}, bf16[256,4096]{1,0:T(8,128)(2,1)S(1)}, u32[]{:S(2)}, u32[]{:S(2)}) collective-permute-start(bf16[256,4096]{1,0:T(8,128)(2,1)} %fusion.5), channel_id=1, source_target_pairs={{0,64},{64,0},{4,68},{68,4},{8,72},{72,8},{12,76},{76,12},{16,80},... | collective-permute-start | bytes 6291464 | tf_op jit(solution)/shard_map/ppermute | solution.py:17
  241.9 4.6 collective-permute-start.6
  246.6 14.8 %collective-permute-start.7 = (bf16[32,4096]{1,0:T(8,128)(2,1)S(1)}, bf16[32,4096]{1,0:T(8,128)(2,1)S(1)}, u32[]{:S(2)}, u32[]{:S(2)}) collective-permute-start(bf16[32,4096]{1,0:T(8,128)(2,1)S(1)} %maximum_select_fusion.21), channel_id=1, source_target_pairs={{0,8},{8,0},{4,12},{12,4},{16,24},{24,16},{20,28},{28,20},{32,40},... | collective-permute-start | bytes 786440 | tf_op jit(solution)/shard_map/ppermute | solution.py:17
  261.5 13.1 %collective-permute-start.8 = (bf16[64,4096]{1,0:T(8,128)(2,1)S(1)}, bf16[64,4096]{1,0:T(8,128)(2,1)S(1)}, u32[]{:S(2)}, u32[]{:S(2)}) collective-permute-start(bf16[64,4096]{1,0:T(8,128)(2,1)S(1)} %maximum_select_fusion.19), channel_id=1, source_target_pairs={{0,16},{16,0},{4,20},{20,4},{8,24},{24,8},{12,28},{28,12},{32,48},... | collective-permute-start | bytes 1572872 | tf_op jit(solution)/shard_map/ppermute | solution.py:17
  274.8 24.9 %collective-permute-start.9 = (bf16[128,4096]{1,0:T(8,128)(2,1)S(1)}, bf16[128,4096]{1,0:T(8,128)(2,1)S(1)}, u32[]{:S(2)}, u32[]{:S(2)}) collective-permute-start(bf16[128,4096]{1,0:T(8,128)(2,1)S(1)} %maximum_select_fusion.16), channel_id=1, source_target_pairs={{0,32},{32,0},{4,36},{36,4},{8,40},{40,8},{12,44},{44,12},{16,48},... | collective-permute-start | bytes 3145736 | tf_op jit(solution)/shard_map/ppermute | solution.py:17
  301.6 53.2 %collective-permute-start.10 = (bf16[256,4096]{1,0:T(8,128)(2,1)}, bf16[256,4096]{1,0:T(8,128)(2,1)}, u32[]{:S(2)}, u32[]{:S(2)}) collective-permute-start(bf16[256,4096]{1,0:T(8,128)(2,1)} %maximum_select_fusion.13), channel_id=1, source_target_pairs={{0,64},{64,0},{4,68},{68,4},{8,72},{72,8},{12,76},{76,12},{16,80},... | collective-permute-start | bytes 6291464 | tf_op jit(solution)/shard_map/ppermute | solution.py:17
  302.4 222.7 %all-reduce.8.cloned.1.call-start = ((), (), s32[]{:S(2)}) async-start(), calls=%async_computation.2 | async-start | bytes 524288 | tf_op jit(solution)/shard_map/psum | solution.py:22
  362.0 49.2 %collective-permute-start.11 = (bf16[256,4096]{1,0:T(8,128)(2,1)}, bf16[256,4096]{1,0:T(8,128)(2,1)S(1)}, u32[]{:S(2)}, u32[]{:S(2)}) collective-permute-start(bf16[256,4096]{1,0:T(8,128)(2,1)} %fusion.4), channel_id=1, source_target_pairs={{0,128},{128,0},{4,132},{132,4},{8,136},{136,8},{12,140},{140,12},... | collective-permute-start | bytes 6291464 | tf_op jit(solution)/shard_map/ppermute | solution.py:17
  415.6 3.2 collective-permute-start.12
  418.8 8.5 %collective-permute-start.13 = (bf16[16,4096]{1,0:T(8,128)(2,1)S(1)}, bf16[16,4096]{1,0:T(8,128)(2,1)S(1)}, u32[]{:S(2)}, u32[]{:S(2)}) collective-permute-start(bf16[16,4096]{1,0:T(8,128)(2,1)S(1)} %maximum_select_fusion.23), channel_id=1, source_target_pairs={{0,8},{8,0},{4,12},{12,4},{16,24},{24,16},{20,28},{28,20},{32,40},... | collective-permute-start | bytes 393224 | tf_op jit(solution)/shard_map/ppermute | solution.py:17
  427.4 7.0 %collective-permute-start.14 = (bf16[32,4096]{1,0:T(8,128)(2,1)S(1)}, bf16[32,4096]{1,0:T(8,128)(2,1)S(1)}, u32[]{:S(2)}, u32[]{:S(2)}) collective-permute-start(bf16[32,4096]{1,0:T(8,128)(2,1)S(1)} %maximum_select_fusion.22), channel_id=1, source_target_pairs={{0,16},{16,0},{4,20},{20,4},{8,24},{24,8},{12,28},{28,12},{32,48},... | collective-permute-start | bytes 786440 | tf_op jit(solution)/shard_map/ppermute | solution.py:17
  434.4 13.2 %collective-permute-start.15 = (bf16[64,4096]{1,0:T(8,128)(2,1)S(1)}, bf16[64,4096]{1,0:T(8,128)(2,1)S(1)}, u32[]{:S(2)}, u32[]{:S(2)}) collective-permute-start(bf16[64,4096]{1,0:T(8,128)(2,1)S(1)} %maximum_select_fusion.20), channel_id=1, source_target_pairs={{0,32},{32,0},{4,36},{36,4},{8,40},{40,8},{12,44},{44,12},{16,48},... | collective-permute-start | bytes 1572872 | tf_op jit(solution)/shard_map/ppermute | solution.py:17
  447.9 22.0 %collective-permute-start.16 = (bf16[128,4096]{1,0:T(8,128)(2,1)S(1)}, bf16[128,4096]{1,0:T(8,128)(2,1)S(1)}, u32[]{:S(2)}, u32[]{:S(2)}) collective-permute-start(bf16[128,4096]{1,0:T(8,128)(2,1)S(1)} %maximum_select_fusion.17), channel_id=1, source_target_pairs={{0,64},{64,0},{4,68},{68,4},{8,72},{72,8},{12,76},{76,12},{16,80},... | collective-permute-start | bytes 3145736 | tf_op jit(solution)/shard_map/ppermute | solution.py:17
  471.8 53.2 %collective-permute-start.17 = (bf16[256,4096]{1,0:T(8,128)(2,1)}, bf16[256,4096]{1,0:T(8,128)(2,1)}, u32[]{:S(2)}, u32[]{:S(2)}) collective-permute-start(bf16[256,4096]{1,0:T(8,128)(2,1)} %maximum_select_fusion.14), channel_id=1, source_target_pairs={{0,128},{128,0},{4,132},{132,4},{8,136},{136,8},{12,140},{140,12},... | collective-permute-start | bytes 6291464 | tf_op jit(solution)/shard_map/ppermute | solution.py:17
Sparse Core Ops, SparseCore 0:
  124.8 57.8 all-reduce.3
  302.5 52.3 all-reduce.5
  472.7 52.3 all-reduce.7
where the time goes:
time: 539 us
  waiting for transfers between devices  446 us (83%)
  matrix products  42.6 us (8%)
  starting transfers between devices  18.4 us (3%)
  between operations  13.4 us (2%)
  other arithmetic  12.3 us (2%)
  local copies, waits for them, and re-layouts  6.04 us (1%)
    ppermute x18, waiting for transfers between devices, swapped(): return lax.ppermute(block, axis, route)  283 us
    psum x3, waiting for transfers between devices, spread(): return lax.psum(block, axis)  163 us
    dot_general x3, matrix products, on_device(): jnp.dot(columns, upper_rows, preferred_element_type=jnp.float32)  21.5 us
    ppermute x18, starting transfers between devices, swapped(): return lax.ppermute(block, axis, route)  18.3 us
    dot_general x3, matrix products, extend_add(): jnp.einsum('sb,brc->src', own_table, own_blocks, preferred_element_type=j...  12.1 us
  transfers between devices with their start and end apart: 21, of which 18 were waited for; matrix products, arithmetic and copies ran while one was open for 3% of the time, Pallas kernels for 0%

commit v1 on v0

--- a/solution.py
+++ b/solution.py
@@ -19,7 +19,7 @@
 
 def spread(block, axis, owner):
     block = jnp.where(lax.axis_index(axis) == owner, block, jnp.zeros_like(block))
-    return lax.psum(block, axis)
+    return jnp.sum(lax.all_gather(block, axis), axis=0)
 
 
 def extend_add(front_slab, partner, own_index, cross_index, block_count):

time: 539 us -> 493 us (0.915); the launches traced: 539 us -> 487 us
  waiting for transfers between devices: 446 us -> 371 us
  starting transfers between devices: 18.4 us -> 37.4 us
    psum x3 -> x0, waiting for transfers between devices: 163 us -> none  [spread(): return lax.psum(block, axis)]
    all_gather x0 -> x3, waiting for transfers between devices: none -> 111 us  [spread(): return jnp.sum(lax.all_gather(block, axis), axis=0)]
    ppermute x18, waiting for transfers between devices: 283 us -> 259 us  [swapped(): return lax.ppermute(block, axis, route)]
    ppermute x18, starting transfers between devices: 18.3 us -> 37.3 us  [swapped(): return lax.ppermute(block, axis, route)]
  transfers between devices with their start and end apart: 21 -> 21, of which waited for: 18 -> 20; matrix products, arithmetic and copies ran while one was open for 3% -> 4% of each run, Pallas kernels for 0% -> 0%
where the time goes in v1:
time: 493 us; the launch traced here: 487 us
  waiting for transfers between devices  371 us (75%)
  matrix products  42.4 us (9%)
  starting transfers between devices  37.4 us (8%)
  other arithmetic  16.7 us (3%)
  between operations  13.4 us (3%)
  local copies, waits for them, and re-layouts  6.04 us (1%)
    ppermute x18, waiting for transfers between devices, swapped(): return lax.ppermute(block, axis, route)  259 us
    all_gather x3, waiting for transfers between devices, spread(): return jnp.sum(lax.all_gather(block, axis), axis=0)  111 us
    ppermute x18, starting transfers between devices, swapped(): return lax.ppermute(block, axis, route)  37.3 us
    dot_general x3, matrix products, on_device(): jnp.dot(columns, upper_rows, preferred_element_type=jnp.float32)  21.2 us
    dot_general x3, matrix products, extend_add(): jnp.einsum('sb,brc->src', own_table, own_blocks, preferred_element_type=j...  12.1 us
    select_n x12, other arithmetic, collect_pivots(): jnp.where(upper_half, jnp.concatenate([received, buffer], axis=0), jnp.co...  10.2 us
  transfers between devices with their start and end apart: 21, of which 20 were waited for; matrix products, arithmetic and copies ran while one was open for 4% of the time, Pallas kernels for 0%

profile of v1, /device:TPU:1, one launch (start us, length us, event | category | flops | bytes accessed | tf_op | source)
XLA Modules:
  0.0 486.6 jit_solution(5400844020995580519)
XLA Ops:
  6.5 3.6 collective-permute-start
  12.1 4.0 fusion.34
  16.2 38.6 %collective-permute-done = bf16[256,4096]{1,0:T(8,128)(2,1)S(1)} collective-permute-done((bf16[256,4096]{1,0:T(8,128)(2,1)}, bf16[256,4096]{1,0:T(8,128)(2,1)S(1)}, u32[]{:S(2)}, u32[]{:S(2)}) %collective-permute-start) | collective-permute-done | bytes 2097184 | tf_op jit(solution)/shard_map/ppermute | solution.py:17
  54.7 3.0 fusion.6
  61.7 5.1 %collective-permute-done.1 = bf16[32,4096]{1,0:T(8,128)(2,1)S(1)} collective-permute-done((bf16[32,4096]{1,0:T(8,128)(2,1)S(1)}, bf16[32,4096]{1,0:T(8,128)(2,1)S(1)}, u32[]{:S(2)}, u32[]{:S(2)}) %collective-permute-start.1) | collective-permute-done | bytes 262176 | tf_op jit(solution)/shard_map/ppermute | solution.py:17
  66.9 3.0 collective-permute-start.2
  69.9 22.6 %collective-permute-done.2 = bf16[64,4096]{1,0:T(8,128)(2,1)} collective-permute-done((bf16[64,4096]{1,0:T(8,128)(2,1)S(1)}, bf16[64,4096]{1,0:T(8,128)(2,1)}, u32[]{:S(2)}, u32[]{:S(2)}) %collective-permute-start.2) | collective-permute-done | bytes 524320 | tf_op jit(solution)/shard_map/ppermute | solution.py:17
  95.7 22.0 %collective-permute-done.3 = bf16[128,4096]{1,0:T(8,128)(2,1)} collective-permute-done((bf16[128,4096]{1,0:T(8,128)(2,1)S(1)}, bf16[128,4096]{1,0:T(8,128)(2,1)}, u32[]{:S(2)}, u32[]{:S(2)}) %collective-permute-start.3) | collective-permute-done | bytes 1048608 | tf_op jit(solution)/shard_map/ppermute | solution.py:17
  117.7 3.6 maximum_select_fusion.12
  124.8 34.9 %all-gather.7.cloned.1.call-done = bf16[1024,512]{1,0:T(8,128)(2,1)} async-done(((bf16[256,512]{1,0:T(8,128)(2,1)}), bf16[1024,512]{1,0:T(8,128)(2,1)}) %all-gather.7.cloned.1.call-update) | async-done | bytes 1048592 | tf_op jit(solution)/shard_map/all_gather | solution.py:22
  161.2 6.5 %collective-permute-done.4 = bf16[256,4096]{1,0:T(8,128)(2,1)} collective-permute-done((bf16[256,4096]{1,0:T(8,128)(2,1)}, bf16[256,4096]{1,0:T(8,128)(2,1)}, u32[]{:S(2)}, u32[]{:S(2)}) %collective-permute-start.4) | collective-permute-done | bytes 2097184 | tf_op jit(solution)/shard_map/ppermute | solution.py:17
  167.7 7.1 %fusion.5 = bf16[256,4096]{1,0:T(8,128)(2,1)} fusion(bf16[256,512]{1,0:T(8,128)(2,1)S(1)} %reduce_sum.36, bf16[256,4096]{1,0:T(8,128)(2,1)S(1)} %bitcast.47, bf16[256,4096]{1,0:T(8,128)(2,1)} %maximum_select_fusion.12, bf16[256,4096]{1,0:T(8,128)(2,1)} %collective-permute-done.4, pred[]{:T(512)S(6)} %eq.139, pred[256]{0:T(512)(128)(4,1)S(1)} %iota_compare_fusion, ...), kind=kOutput, calls=%fused_computation.14 | convolution fusion | flops 3246391296 | bytes 9175301 | tf_op jit(solution)/shard_map/dot_general | solution.py:85
  176.1 4.1 fusion.31
  180.1 38.6 %collective-permute-done.5 = bf16[256,4096]{1,0:T(8,128)(2,1)S(1)} collective-permute-done((bf16[256,4096]{1,0:T(8,128)(2,1)}, bf16[256,4096]{1,0:T(8,128)(2,1)S(1)}, u32[]{:S(2)}, u32[]{:S(2)}) %collective-permute-start.5) | collective-permute-done | bytes 2097184 | tf_op jit(solution)/shard_map/ppermute | solution.py:17
  218.8 3.0 fusion.7
  223.1 5.0 %collective-permute-start.6 = (bf16[16,4096]{1,0:T(8,128)(2,1)S(1)}, bf16[16,4096]{1,0:T(8,128)(2,1)S(1)}, u32[]{:S(2)}, u32[]{:S(2)}) collective-permute-start(bf16[16,4096]{1,0:T(8,128)(2,1)S(1)} %slice.51), channel_id=1, source_target_pairs={{0,4},{4,0},{8,12},{12,8},{16,20},{20,16},{24,28},{28,24},{32,36},... | collective-permute-start | bytes 393224 | tf_op jit(solution)/shard_map/ppermute | solution.py:17
  230.5 3.3 collective-permute-start.7
  233.7 10.1 %collective-permute-done.7 = bf16[32,4096]{1,0:T(8,128)(2,1)S(1)} collective-permute-done((bf16[32,4096]{1,0:T(8,128)(2,1)S(1)}, bf16[32,4096]{1,0:T(8,128)(2,1)S(1)}, u32[]{:S(2)}, u32[]{:S(2)}) %collective-permute-start.7) | collective-permute-done | bytes 262176 | tf_op jit(solution)/shard_map/ppermute | solution.py:17
  245.2 9.5 %collective-permute-done.8 = bf16[64,4096]{1,0:T(8,128)(2,1)S(1)} collective-permute-done((bf16[64,4096]{1,0:T(8,128)(2,1)S(1)}, bf16[64,4096]{1,0:T(8,128)(2,1)S(1)}, u32[]{:S(2)}, u32[]{:S(2)}) %collective-permute-start.8) | collective-permute-done | bytes 524320 | tf_op jit(solution)/shard_map/ppermute | solution.py:17
  257.8 21.6 %collective-permute-done.9 = bf16[128,4096]{1,0:T(8,128)(2,1)S(1)} collective-permute-done((bf16[128,4096]{1,0:T(8,128)(2,1)S(1)}, bf16[128,4096]{1,0:T(8,128)(2,1)S(1)}, u32[]{:S(2)}, u32[]{:S(2)}) %collective-permute-start.9) | collective-permute-done | bytes 1048608 | tf_op jit(solution)/shard_map/ppermute | solution.py:17
  283.3 33.6 %all-gather.9.cloned.1.call-done = bf16[1024,512]{1,0:T(8,128)(2,1)} async-done(((bf16[256,512]{1,0:T(8,128)(2,1)}), bf16[1024,512]{1,0:T(8,128)(2,1)}) %all-gather.9.cloned.1.call-update) | async-done | bytes 1048592 | tf_op jit(solution)/shard_map/all_gather | solution.py:22
  318.4 6.7 %collective-permute-done.10 = bf16[256,4096]{1,0:T(8,128)(2,1)} collective-permute-done((bf16[256,4096]{1,0:T(8,128)(2,1)}, bf16[256,4096]{1,0:T(8,128)(2,1)}, u32[]{:S(2)}, u32[]{:S(2)}) %collective-permute-start.10) | collective-permute-done | bytes 2097184 | tf_op jit(solution)/shard_map/ppermute | solution.py:17
  325.1 7.1 %fusion.4 = bf16[256,4096]{1,0:T(8,128)(2,1)} fusion(bf16[256,512]{1,0:T(8,128)(2,1)S(1)} %reduce_sum.37, bf16[256,4096]{1,0:T(8,128)(2,1)S(1)} %bitcast.50, bf16[256,4096]{1,0:T(8,128)(2,1)} %maximum_select_fusion.13, bf16[256,4096]{1,0:T(8,128)(2,1)} %collective-permute-done.10, pred[]{:T(512)S(6)} %eq.147, pred[256]{0:T(512)(128)(4,1)S(1)} %iota_compare_fusion.1, ...), kind=kOutput, calls=%fused_computation.13 | convolution fusion | flops 3246391296 | bytes 9175301 | tf_op jit(solution)/shard_map/dot_general | solution.py:85
  335.0 4.1 fusion.28
  339.1 37.4 %collective-permute-done.11 = bf16[256,4096]{1,0:T(8,128)(2,1)S(1)} collective-permute-done((bf16[256,4096]{1,0:T(8,128)(2,1)}, bf16[256,4096]{1,0:T(8,128)(2,1)S(1)}, u32[]{:S(2)}, u32[]{:S(2)}) %collective-permute-start.11) | collective-permute-done | bytes 2097184 | tf_op jit(solution)/shard_map/ppermute | solution.py:17
  376.4 3.0 fusion.8
  386.2 4.1 collective-permute-done.13
  390.4 5.5 %collective-permute-done.14 = bf16[32,4096]{1,0:T(8,128)(2,1)S(1)} collective-permute-done((bf16[32,4096]{1,0:T(8,128)(2,1)S(1)}, bf16[32,4096]{1,0:T(8,128)(2,1)S(1)}, u32[]{:S(2)}, u32[]{:S(2)}) %collective-permute-start.14) | collective-permute-done | bytes 262176 | tf_op jit(solution)/shard_map/ppermute | solution.py:17
  396.1 11.7 %collective-permute-done.15 = bf16[64,4096]{1,0:T(8,128)(2,1)S(1)} collective-permute-done((bf16[64,4096]{1,0:T(8,128)(2,1)S(1)}, bf16[64,4096]{1,0:T(8,128)(2,1)S(1)}, u32[]{:S(2)}, u32[]{:S(2)}) %collective-permute-start.15) | collective-permute-done | bytes 524320 | tf_op jit(solution)/shard_map/ppermute | solution.py:17
  409.3 14.2 %collective-permute-done.16 = bf16[128,4096]{1,0:T(8,128)(2,1)S(1)} collective-permute-done((bf16[128,4096]{1,0:T(8,128)(2,1)S(1)}, bf16[128,4096]{1,0:T(8,128)(2,1)S(1)}, u32[]{:S(2)}, u32[]{:S(2)}) %collective-permute-start.16) | collective-permute-done | bytes 1048608 | tf_op jit(solution)/shard_map/ppermute | solution.py:17
  428.8 42.8 %all-gather.11.cloned.1.call-done = bf16[1024,512]{1,0:T(8,128)(2,1)} async-done(((bf16[256,512]{1,0:T(8,128)(2,1)}), bf16[1024,512]{1,0:T(8,128)(2,1)}) %all-gather.11.cloned.1.call-update) | async-done | bytes 1048592 | tf_op jit(solution)/shard_map/all_gather | solution.py:22
  473.0 7.0 %fusion.3 = bf16[256,4096]{1,0:T(8,128)(2,1)} fusion(bf16[256,512]{1,0:T(8,128)(2,1)S(1)} %reduce_sum.38, bf16[256,4096]{1,0:T(8,128)(2,1)S(1)} %bitcast.53, bf16[256,4096]{1,0:T(8,128)(2,1)} %maximum_select_fusion.14, bf16[256,4096]{1,0:T(8,128)(2,1)} %collective-permute-done.17, pred[]{:T(512)S(6)} %eq.152, pred[256]{0:T(512)(128)(4,1)S(1)} %iota_compare_fusion.2, ...), kind=kOutput, calls=%fused_computation.12 | convolution fusion | flops 3246391296 | bytes 9175301 | tf_op jit(solution)/shard_map/dot_general | solution.py:85
  (53 shorter events, 47.1 us)
Async XLA Ops:
  6.5 153.2 %all-gather.7.cloned.1.call-start = ((), (), s32[]{:S(2)}) async-start(), calls=%async_computation | async-start | bytes 1310720 | tf_op jit(solution)/shard_map/all_gather | solution.py:22
  6.5 48.2 %collective-permute-start = (bf16[256,4096]{1,0:T(8,128)(2,1)}, bf16[256,4096]{1,0:T(8,128)(2,1)S(1)}, u32[]{:S(2)}, u32[]{:S(2)}) collective-permute-start(bf16[256,4096]{1,0:T(8,128)(2,1)} %param.4), channel_id=1, source_target_pairs={{0,32},{32,0},{4,36},{36,4},{8,40},{40,8},{12,44},{44,12},{16,48},... | collective-permute-start | bytes 6291464 | tf_op jit(solution)/shard_map/ppermute | solution.py:17
  59.1 7.7 %collective-permute-start.1 = (bf16[32,4096]{1,0:T(8,128)(2,1)S(1)}, bf16[32,4096]{1,0:T(8,128)(2,1)S(1)}, u32[]{:S(2)}, u32[]{:S(2)}) collective-permute-start(bf16[32,4096]{1,0:T(8,128)(2,1)S(1)} %slice.49), channel_id=1, source_target_pairs={{0,4},{4,0},{8,12},{12,8},{16,20},{20,16},{24,28},{28,24},{32,36},... | collective-permute-start | bytes 786440 | tf_op jit(solution)/shard_map/ppermute | solution.py:17
  66.9 3.0 copy-start
  66.9 25.6 %collective-permute-start.2 = (bf16[64,4096]{1,0:T(8,128)(2,1)S(1)}, bf16[64,4096]{1,0:T(8,128)(2,1)}, u32[]{:S(2)}, u32[]{:S(2)}) collective-permute-start(bf16[64,4096]{1,0:T(8,128)(2,1)S(1)} %maximum_select_fusion.18), channel_id=1, source_target_pairs={{0,8},{8,0},{4,12},{12,4},{16,24},{24,16},{20,28},{28,20},{32,40},... | collective-permute-start | bytes 1572872 | tf_op jit(solution)/shard_map/ppermute | solution.py:17
  94.4 23.3 %collective-permute-start.3 = (bf16[128,4096]{1,0:T(8,128)(2,1)S(1)}, bf16[128,4096]{1,0:T(8,128)(2,1)}, u32[]{:S(2)}, u32[]{:S(2)}) collective-permute-start(bf16[128,4096]{1,0:T(8,128)(2,1)S(1)} %maximum_select_fusion.15), channel_id=1, source_target_pairs={{0,16},{16,0},{4,20},{20,4},{8,24},{24,8},{12,28},{28,12},{32,48},... | collective-permute-start | bytes 3145736 | tf_op jit(solution)/shard_map/ppermute | solution.py:17
  121.2 46.5 %collective-permute-start.4 = (bf16[256,4096]{1,0:T(8,128)(2,1)}, bf16[256,4096]{1,0:T(8,128)(2,1)}, u32[]{:S(2)}, u32[]{:S(2)}) collective-permute-start(bf16[256,4096]{1,0:T(8,128)(2,1)} %maximum_select_fusion.12), channel_id=1, source_target_pairs={{0,32},{32,0},{4,36},{36,4},{8,40},{40,8},{12,44},{44,12},{16,48},... | collective-permute-start | bytes 6291464 | tf_op jit(solution)/shard_map/ppermute | solution.py:17
  124.7 192.2 %all-gather.9.cloned.1.call-start = ((), (), s32[]{:S(2)}) async-start(), calls=%async_computation.1 | async-start | bytes 1310720 | tf_op jit(solution)/shard_map/all_gather | solution.py:22
  174.8 43.9 %collective-permute-start.5 = (bf16[256,4096]{1,0:T(8,128)(2,1)}, bf16[256,4096]{1,0:T(8,128)(2,1)S(1)}, u32[]{:S(2)}, u32[]{:S(2)}) collective-permute-start(bf16[256,4096]{1,0:T(8,128)(2,1)} %fusion.5), channel_id=1, source_target_pairs={{0,64},{64,0},{4,68},{68,4},{8,72},{72,8},{12,76},{76,12},{16,80},... | collective-permute-start | bytes 6291464 | tf_op jit(solution)/shard_map/ppermute | solution.py:17
  223.1 7.3 %collective-permute-start.6 = (bf16[16,4096]{1,0:T(8,128)(2,1)S(1)}, bf16[16,4096]{1,0:T(8,128)(2,1)S(1)}, u32[]{:S(2)}, u32[]{:S(2)}) collective-permute-start(bf16[16,4096]{1,0:T(8,128)(2,1)S(1)} %slice.51), channel_id=1, source_target_pairs={{0,4},{4,0},{8,12},{12,8},{16,20},{20,16},{24,28},{28,24},{32,36},... | collective-permute-start | bytes 393224 | tf_op jit(solution)/shard_map/ppermute | solution.py:17
  230.5 13.4 %collective-permute-start.7 = (bf16[32,4096]{1,0:T(8,128)(2,1)S(1)}, bf16[32,4096]{1,0:T(8,128)(2,1)S(1)}, u32[]{:S(2)}, u32[]{:S(2)}) collective-permute-start(bf16[32,4096]{1,0:T(8,128)(2,1)S(1)} %maximum_select_fusion.21), channel_id=1, source_target_pairs={{0,8},{8,0},{4,12},{12,4},{16,24},{24,16},{20,28},{28,20},{32,40},... | collective-permute-start | bytes 786440 | tf_op jit(solution)/shard_map/ppermute | solution.py:17
  244.0 10.7 %collective-permute-start.8 = (bf16[64,4096]{1,0:T(8,128)(2,1)S(1)}, bf16[64,4096]{1,0:T(8,128)(2,1)S(1)}, u32[]{:S(2)}, u32[]{:S(2)}) collective-permute-start(bf16[64,4096]{1,0:T(8,128)(2,1)S(1)} %maximum_select_fusion.19), channel_id=1, source_target_pairs={{0,16},{16,0},{4,20},{20,4},{8,24},{24,8},{12,28},{28,12},{32,48},... | collective-permute-start | bytes 1572872 | tf_op jit(solution)/shard_map/ppermute | solution.py:17
  255.0 24.4 %collective-permute-start.9 = (bf16[128,4096]{1,0:T(8,128)(2,1)S(1)}, bf16[128,4096]{1,0:T(8,128)(2,1)S(1)}, u32[]{:S(2)}, u32[]{:S(2)}) collective-permute-start(bf16[128,4096]{1,0:T(8,128)(2,1)S(1)} %maximum_select_fusion.16), channel_id=1, source_target_pairs={{0,32},{32,0},{4,36},{36,4},{8,40},{40,8},{12,44},{44,12},{16,48},... | collective-permute-start | bytes 3145736 | tf_op jit(solution)/shard_map/ppermute | solution.py:17
  281.3 43.8 %collective-permute-start.10 = (bf16[256,4096]{1,0:T(8,128)(2,1)}, bf16[256,4096]{1,0:T(8,128)(2,1)}, u32[]{:S(2)}, u32[]{:S(2)}) collective-permute-start(bf16[256,4096]{1,0:T(8,128)(2,1)} %maximum_select_fusion.13), channel_id=1, source_target_pairs={{0,64},{64,0},{4,68},{68,4},{8,72},{72,8},{12,76},{76,12},{16,80},... | collective-permute-start | bytes 6291464 | tf_op jit(solution)/shard_map/ppermute | solution.py:17
  283.3 188.3 %all-gather.11.cloned.1.call-start = ((), (), s32[]{:S(2)}) async-start(), calls=%async_computation.2 | async-start | bytes 1310720 | tf_op jit(solution)/shard_map/all_gather | solution.py:22
  332.2 44.3 %collective-permute-start.11 = (bf16[256,4096]{1,0:T(8,128)(2,1)}, bf16[256,4096]{1,0:T(8,128)(2,1)S(1)}, u32[]{:S(2)}, u32[]{:S(2)}) collective-permute-start(bf16[256,4096]{1,0:T(8,128)(2,1)} %fusion.4), channel_id=1, source_target_pairs={{0,128},{128,0},{4,132},{132,4},{8,136},{136,8},{12,140},{140,12},... | collective-permute-start | bytes 6291464 | tf_op jit(solution)/shard_map/ppermute | solution.py:17
  380.8 3.2 collective-permute-start.12
  384.0 6.3 %collective-permute-start.13 = (bf16[16,4096]{1,0:T(8,128)(2,1)S(1)}, bf16[16,4096]{1,0:T(8,128)(2,1)S(1)}, u32[]{:S(2)}, u32[]{:S(2)}) collective-permute-start(bf16[16,4096]{1,0:T(8,128)(2,1)S(1)} %maximum_select_fusion.23), channel_id=1, source_target_pairs={{0,8},{8,0},{4,12},{12,4},{16,24},{24,16},{20,28},{28,20},{32,40},... | collective-permute-start | bytes 393224 | tf_op jit(solution)/shard_map/ppermute | solution.py:17
  390.3 5.6 %collective-permute-start.14 = (bf16[32,4096]{1,0:T(8,128)(2,1)S(1)}, bf16[32,4096]{1,0:T(8,128)(2,1)S(1)}, u32[]{:S(2)}, u32[]{:S(2)}) collective-permute-start(bf16[32,4096]{1,0:T(8,128)(2,1)S(1)} %maximum_select_fusion.22), channel_id=1, source_target_pairs={{0,16},{16,0},{4,20},{20,4},{8,24},{24,8},{12,28},{28,12},{32,48},... | collective-permute-start | bytes 786440 | tf_op jit(solution)/shard_map/ppermute | solution.py:17
  396.0 11.8 %collective-permute-start.15 = (bf16[64,4096]{1,0:T(8,128)(2,1)S(1)}, bf16[64,4096]{1,0:T(8,128)(2,1)S(1)}, u32[]{:S(2)}, u32[]{:S(2)}) collective-permute-start(bf16[64,4096]{1,0:T(8,128)(2,1)S(1)} %maximum_select_fusion.20), channel_id=1, source_target_pairs={{0,32},{32,0},{4,36},{36,4},{8,40},{40,8},{12,44},{44,12},{16,48},... | collective-permute-start | bytes 1572872 | tf_op jit(solution)/shard_map/ppermute | solution.py:17
  408.1 15.5 %collective-permute-start.16 = (bf16[128,4096]{1,0:T(8,128)(2,1)S(1)}, bf16[128,4096]{1,0:T(8,128)(2,1)S(1)}, u32[]{:S(2)}, u32[]{:S(2)}) collective-permute-start(bf16[128,4096]{1,0:T(8,128)(2,1)S(1)} %maximum_select_fusion.17), channel_id=1, source_target_pairs={{0,64},{64,0},{4,68},{68,4},{8,72},{72,8},{12,76},{76,12},{16,80},... | collective-permute-start | bytes 3145736 | tf_op jit(solution)/shard_map/ppermute | solution.py:17
  425.5 47.5 %collective-permute-start.17 = (bf16[256,4096]{1,0:T(8,128)(2,1)}, bf16[256,4096]{1,0:T(8,128)(2,1)}, u32[]{:S(2)}, u32[]{:S(2)}) collective-permute-start(bf16[256,4096]{1,0:T(8,128)(2,1)} %maximum_select_fusion.14), channel_id=1, source_target_pairs={{0,128},{128,0},{4,132},{132,4},{8,136},{136,8},{12,140},{140,12},... | collective-permute-start | bytes 6291464 | tf_op jit(solution)/shard_map/ppermute | solution.py:17
Sparse Core Ops, SparseCore 0:
  124.9 34.8 all-gather.6
  283.4 33.4 all-gather.8
  428.9 42.6 all-gather.10
